TPU v7x, 512 devices: a whole 4x4x16 slice. The times are simulated.
512 devices in a mesh: section: 4 (over z_hi), vocab: 32 (over z_lo, y, core), dp: 4 (over x).
Axes of the slice: x: 4, y: 4, z: 16 (z_hi: 4, z_lo: 4; z = z_hi * 4 + z_lo), core: 2. Of those that a mesh axis runs over, the one named last changes fastest.
Arguments:
- features: bfloat16 [4, 128, 32, 3072], P('dp', 'vocab', None, 'section'), may hold values from -6 to 6
- dw_weight: float32 [7, 7, 3072], P(None, None, 'section'), may hold values from -1.75 to 1.75
- ln_gain: float32 [3072], P('section'), may hold values from 0.25 to 1.75
- ln_bias: float32 [3072], P('section'), may hold values from -3 to 3
- layer_scale: float32 [3072], P('section'), may hold values from 0.25 to 2
- proj_weight: bfloat16 [3072, 8192], P('section', 'vocab'), may hold values from -0.109375 to 0.109375
- text_embed: bfloat16 [4, 512, 8192], P('dp', 'section', 'vocab'), may hold values from -6 to 6
- positions: int32 [4, 256], P('dp'), may hold values from 0 to 511, as said below
- rms_gain: float32 [8192], replicated, may hold values from 0.25 to 1.75
- head_weight: bfloat16 [8192, 64128], P('dp', ('section', 'vocab'))
- labels: int32 [4, 512], P('dp'), may hold values from 0 to 64127
Outputs:
- visual: bfloat16 [4, 256, 3072], P('dp', 'vocab', 'section')
- loss: float32 [4, 512], P('dp', 'section')
Inputs may be any that keep to these rules, and one draw needn't show every extreme that they name: The positions of one sequence are distinct.
All inputs are finite; a program needn't handle non-finite values.
Results may differ from a plain program's by a relative error of at most 0.008.
Values may be sent and summed in bfloat16 or wider, within the bound.
No kernel may reach another device: no remote copies, remote signals or barrier semaphores. Data moves between devices by JAX's collectives and lax.ppermute only.
A program may use at most 64 MiB of HBM per device.

v0:
```python
import functools

import jax
import jax.numpy as jnp
from jax import lax
from jax.experimental import pallas as pl
from jax.experimental.pallas import tpu as pltpu
from jax.sharding import PartitionSpec as P

WIDE = 256
LOW = 160
VOCAB = ("zl", "y", "core")


def shifted(value, axis, step):
    count = lax.axis_size(axis)
    return lax.ppermute(value, axis, [((i + step) % count, i) for i in range(count)])


def extended(cells, axis, width):
    count = lax.axis_size(axis)
    ends = count - 1
    head, tail = cells[:width], cells[-width:]
    return jnp.concatenate(
        [
            lax.ppermute(tail, axis, [(i, (i + 1) % count) for i in range(ends)]),
            cells,
            lax.ppermute(head, axis, [((i + 1) % count, i) for i in range(ends)]),
        ],
        axis=0,
    )


def head_kernel(columns, offsets, from_text, own_ref, gain_ref, meta_ref, *refs):
    x_v, w_v, scaled, total, squares, sem_x, sem_w = refs[-7:]
    out_ref = refs[-8]
    w_low, w_own, w_left, w_right, w_far, w_off = refs[-14:-8]
    parts, lines, cores, rows, width = x_v.shape
    own, core = own_ref[0], own_ref[1]

    def block(j):
        return lax.rem(own + offsets[j], parts)

    def x_copies(j):
        if from_text:
            return [pltpu.make_async_copy(refs[0].at[block(j)], x_v.at[j], sem_x.at[j, 0])]
        return [
            pltpu.make_async_copy(
                refs[k].at[:, block(j)],
                x_v.at[j, :, core if k == 0 else 1 - core],
                sem_x.at[j, k],
            )
            for k in range(2)
        ]

    def w_copies(j):
        copies = [
            pltpu.make_async_copy(
                w_low.at[block(j)], w_v.at[j, pl.ds(0, LOW)], sem_w.at[j, 0]
            )
        ]
        if j < 3:
            pieces = ((w_own, w_left, w_right)[j],)
        else:
            pieces = (w_far, w_off)
        size = (2 * WIDE - LOW) // len(pieces)
        for k, piece in enumerate(pieces):
            copies.append(
                pltpu.make_async_copy(
                    piece, w_v.at[j, pl.ds(LOW + k * size, size)], sem_w.at[j, k + 1]
                )
            )
        return copies

    for j in range(parts):
        for copy in x_copies(j) + w_copies(j):
            copy.start()
    for j in range(parts):
        for copy in x_copies(j):
            copy.wait()
        sums = jnp.zeros((rows, width), jnp.float32)
        for line in range(lines):
            for at in range(cores):
                piece = line * cores + at
                wide = x_v[j, line, at].astype(jnp.float32)
                sums = sums + wide * wide
                gain = gain_ref[block(j) * (lines * cores) + piece]
                scaled[:, piece * width : (piece + 1) * width] = (wide * gain).astype(
                    jnp.bfloat16
                )
        for copy in w_copies(j):
            copy.wait()
        part = lax.dot_general(
            scaled[...], w_v[j], (((1,), (1,)), ((), ())), preferred_element_type=jnp.float32
        )
        sums = jnp.sum(sums, axis=1, keepdims=True)
        if j == 0:
            total[...] = part
            squares[...] = sums
        else:
            total[...] += part
            squares[...] += sums
    factor = lax.rsqrt(squares[...] / (parts * lines * cores * width) + 1e-05)
    logits = total[...] * factor
    at = lax.broadcasted_iota(jnp.int32, logits.shape, 1)
    real = at < columns
    top = jnp.max(jnp.where(real, logits, -jnp.inf), axis=1, keepdims=True)
    summed = jnp.sum(
        jnp.where(real, jnp.exp(logits - top), 0.0), axis=1, keepdims=True
    )
    chosen = jnp.sum(
        jnp.where((at == meta_ref[:, 1:2]) & real, logits, 0.0), axis=1, keepdims=True
    )
    hit = (
        lax.broadcasted_iota(jnp.int32, (rows, out_ref.shape[1]), 1) == meta_ref[:, 0:1]
    )
    out_ref[...] = jnp.zeros(out_ref.shape, jnp.float32)
    for k, value in enumerate((top, summed, chosen)):
        out_ref[k : k + 1, :] = jnp.sum(jnp.where(hit, value, 0.0), axis=0, keepdims=True)


def head_stats(own, gain, meta, xs, weights, dep, columns, offsets, places):
    from_text = len(xs) == 1
    rows = meta.shape[0]
    parts, lines, cores = len(offsets), 4, 2
    width = xs[0].shape[-1]
    depth = lines * cores * width
    vmem = pl.BlockSpec(memory_space=pltpu.VMEM)
    anywhere = pl.BlockSpec(memory_space=pl.ANY)
    return pl.pallas_call(
        functools.partial(head_kernel, columns, offsets, from_text),
        out_shape=jax.ShapeDtypeStruct((8, places), jnp.float32),
        in_specs=[pl.BlockSpec(memory_space=pltpu.SMEM), vmem, vmem]
        + [anywhere] * (len(xs) + len(dep) + len(weights)),
        out_specs=vmem,
        scratch_shapes=[
            pltpu.VMEM((parts, lines, cores, rows, width), jnp.bfloat16),
            pltpu.VMEM((parts, 2 * WIDE, depth), jnp.bfloat16),
            pltpu.VMEM((rows, depth), jnp.bfloat16),
            pltpu.VMEM((rows, 2 * WIDE), jnp.float32),
            pltpu.VMEM((rows, 1), jnp.float32),
            pltpu.SemaphoreType.DMA((parts, 2)),
            pltpu.SemaphoreType.DMA((parts, 3)),
        ],
        compiler_params=pltpu.CompilerParams(vmem_limit_bytes=56 * 1024 * 1024),
        cost_estimate=pl.CostEstimate(
            flops=4 * rows * WIDE * parts * depth,
            bytes_accessed=2 * parts * depth * (rows + 2 * WIDE),
            transcendentals=2 * rows * WIDE,
        ),
    )(own, gain, meta, *xs, *dep, *weights)


def across(value, turn):
    count = lax.axis_size("section")
    pairs = [(i, i ^ 1) if turn == 0 else (i, count - 1 - i) for i in range(count)]
    return lax.ppermute(value, "section", pairs)


def to_all(value, axis):
    count = lax.axis_size(axis)
    return lax.all_to_all(jnp.broadcast_to(value[None], (count,) + value.shape), axis, 0, 0)


def shards(
    features,
    dw_weight,
    ln_gain,
    ln_bias,
    layer_scale,
    proj_weight,
    text_embed,
    positions,
    rms_gain,
    head_weight,
    labels,
):
    sections = lax.axis_size("section")
    parts = lax.axis_size("dp")
    shard_index = lax.axis_index(("section",) + VOCAB)
    places = positions[0]
    targets = labels[0]
    columns = head_weight.shape[1]
    slots = lax.iota(jnp.int32, targets.shape[0])

    text = to_all(text_embed[0], "section").reshape(slots.shape[0], -1)

    weight = head_weight.T
    low_all = lax.all_gather(weight[:LOW], "dp", axis=0)
    high = jnp.pad(weight[LOW:], ((0, 2 * WIDE - columns), (0, 0)))
    left, right = shifted(high, "dp", -1), shifted(high, "dp", 1)

    image = features[0]
    height, width, chans = image.shape
    padded = extended(image, VOCAB, 3)
    padded = jnp.pad(padded, ((0, 0), (3, 3), (0, 0))).astype(jnp.float32)
    conv = jnp.zeros((height, width, chans), jnp.float32)
    for row_off in range(7):
        for col_off in range(7):
            conv = (
                conv
                + padded[row_off : row_off + height, col_off : col_off + width]
                * dw_weight[row_off, col_off]
            )
    sums = jnp.stack(
        [jnp.sum(conv, axis=-1).reshape(-1), jnp.sum(conv * conv, axis=-1).reshape(-1)]
    )
    sums = lax.psum(sums, "section")

    is_text = jnp.all(slots[:, None] != places[None, :], axis=1)
    rank = jnp.sum(
        jnp.where((slots[None, :] < slots[:, None]) & is_text[None, :], 1, 0), axis=1
    )
    text_rows = slots.shape[0] - places.shape[0]
    select = (rank[None, :] == lax.iota(jnp.int32, text_rows)[:, None]) & is_text[None, :]
    text, _, _ = lax.optimization_barrier((text, sums, low_all))
    text = jnp.dot(
        select.astype(jnp.bfloat16), text, preferred_element_type=jnp.float32
    ).astype(jnp.bfloat16)
    text_slots = jnp.sum(jnp.where(select, slots[None, :], 0), axis=1)
    text_all = lax.all_gather(text, VOCAB, axis=0)
    text_all = text_all.reshape(tuple(lax.axis_size(axis) for axis in VOCAB) + text.shape)
    all_chans = chans * sections
    middle = sums[0].reshape(height, width) / all_chans
    spread = sums[1].reshape(height, width) / all_chans - middle * middle
    normal = (conv - middle[..., None]) * lax.rsqrt(spread + 1e-06)[..., None] * ln_gain + ln_bias
    block = image.astype(jnp.float32) + layer_scale * normal
    pooled = block.reshape(height // 4, 4, width // 4, 4, chans).mean(axis=(1, 3))
    pooled = pooled.reshape(-1, chans).astype(jnp.bfloat16)

    tokens = to_all(pooled, VOCAB).reshape(-1, chans)
    rows = jnp.dot(tokens, proj_weight, preferred_element_type=jnp.float32)
    for turn in range(2):
        rows = rows + across(rows.astype(jnp.bfloat16), turn).astype(jnp.float32)
    rows = rows.astype(jnp.bfloat16)

    rows, left, right = lax.optimization_barrier((rows, left, right))
    half = high.shape[0] // 2
    far, off = shifted(left[:half], "dp", -1), shifted(right[half:], "dp", 1)
    rows = to_all(rows, "zl")
    rows, text_all = lax.optimization_barrier((rows, text_all))
    early = rows
    rows = to_all(rows, "y")
    rows, far, off, low_all = lax.optimization_barrier((rows, far, off, low_all))
    partner = lax.ppermute(rows, "core", [(0, 1), (1, 0)])

    gain = rms_gain.reshape(-1, 1, text.shape[1])
    own = jnp.stack([lax.axis_index("dp"), lax.axis_index("core")])
    offsets = (0, parts - 1, 1, 2)

    def stats(at, xs, dep):
        ids = jnp.sum(jnp.where(at[:, None] == slots[None, :], targets[None, :], 0), axis=1)
        ids = ids - shard_index * columns
        return head_stats(
            own,
            gain,
            jnp.stack([at, ids], axis=1),
            xs,
            (low_all, high, left, right, far, off),
            dep,
            columns,
            offsets,
            targets.shape[0],
        )

    of_text = stats(text_slots, (text_all,), (early,))
    of_visual = stats(places, (rows, partner), ())
    both = (of_text + of_visual)[:3]

    def merged(pieces):
        tops, totals, chosen = pieces[:, 0], pieces[:, 1], pieces[:, 2]
        top = jnp.max(tops, axis=0)
        return jnp.stack(
            [top, jnp.sum(totals * jnp.exp(tops - top), axis=0), jnp.sum(chosen, axis=0)]
        )

    for turn in range(2):
        both = merged(jnp.stack([both, across(both, turn)]))
    both = both.reshape(3, sections, -1)
    both = lax.dynamic_index_in_dim(both, lax.axis_index("section"), 1, keepdims=False)
    top, total, chosen = merged(to_all(both, VOCAB))
    loss = top + jnp.log(total) - chosen
    return (pooled[None], loss[None])


def solution(mesh):
    in_specs = (
        P("dp", VOCAB, None, "section"),
        P(None, None, "section"),
        P("section"),
        P("section"),
        P("section"),
        P("section", VOCAB),
        P("dp", "section", VOCAB),
        P("dp", None),
        P(),
        P("dp", ("section",) + VOCAB),
        P("dp", None),
    )
    out_specs = (P("dp", VOCAB, "section"), P("dp", "section"))
    sizes = (mesh.shape["section"], mesh.shape["vocab"] // 8, 4, 2, mesh.shape["dp"])
    mesh = jax.sharding.Mesh(mesh.devices.reshape(sizes), ("section",) + VOCAB + ("dp",))
    return jax.shard_map(shards, mesh=mesh, in_specs=in_specs, out_specs=out_specs, check_vma=False)
```

profile of v0, /device:TPU:1, one launch (start us, length us, event | category | flops | bytes accessed | tf_op | source)
XLA Modules:
  0.0 243.8 jit_solution(11282447047430177858)
XLA Ops:
  9.4 4.7 %collective-permute-start = (bf16[3,32,768]{2,1,0:T(8,128)(2,1)S(1)}, bf16[3,32,768]{2,1,0:T(8,128)(2,1)S(1)}, u32[]{:S(2)}, u32[]{:S(2)}) collective-permute-start(bf16[3,32,768]{2,1,0:T(8,128)(2,1)S(1)} %get-tuple-element.82), channel_id=1, source_target_pairs={{0,4},{4,8},{8,12},{12,16},{16,20},{20,24},{24,28},{28,32},{32,36}... | collective-permute-start | bytes 442376 | tf_op jit(solution)/shard_map/ppermute | solution.py:26
  14.1 5.5 %collective-permute-start.1 = (bf16[3,32,768]{2,1,0:T(8,128)(2,1)S(1)}, bf16[3,32,768]{2,1,0:T(8,128)(2,1)S(1)}, u32[]{:S(2)}, u32[]{:S(2)}) collective-permute-start(bf16[3,32,768]{2,1,0:T(8,128)(2,1)S(1)} %get-tuple-element.83), channel_id=1, source_target_pairs={{4,0},{8,4},{12,8},{16,12},{20,16},{24,20},{28,24},{32,28},{36,32}... | collective-permute-start | bytes 442376 | tf_op jit(solution)/shard_map/ppermute | solution.py:28
  20.3 11.2 %all-to-all-start.2 = ((bf16[4,128,256]{2,1,0:T(8,128)(2,1)}), bf16[4,128,256]{2,1,0:T(8,128)(2,1)S(1)}, u32[]{:S(2)}, u32[]{:S(2)}) async-start(bf16[4,128,256]{2,1,0:T(8,128)(2,1)} %broadcast_in_dim.100), calls=%async_computation.2 | async-start | bytes 524288 | tf_op jit(solution)/shard_map/all_to_all | solution.py:162
  32.5 4.3 %fusion.79 = (f32[4,32]{1,0:T(4,128)S(1)}, f32[4,32]{1,0:T(4,128)S(1)}, f32[4,32,768]{2,1,0:T(8,128)S(1)}) fusion(f32[768]{0:T(1024)S(1)} %get-tuple-element.71, f32[10,38,768]{2,1,0:T(8,128)S(1)} %fusion.7, f32[768]{0:T(1024)S(1)} %get-tuple-element.72, f32[768]{0:T(1024)S(1)} %get-tuple-element.25, f32[768]{0:T(1024)S(1)} %get-tuple-element.26, ...), kind=kLoop, calls=%fused_computation.221 | loop fusion | flops 9830144 | bytes 19812352 | tf_op jit(solution)/shard_map/reduce_sum | solution.py:206
  37.0 16.1 %psum.7 = f32[2,128]{1,0:T(2,128)S(1)} all-reduce(f32[2,128]{1,0:T(2,128)S(1)} %pad_maximum_fusion.5), channel_id=1, replica_groups=mesh['section'=4,'zl'=4,'y'=4,'core'=2,'dp'=4] {'section'}, use_global_device_ids=true, to_apply=%region_2.3 | all-reduce | flops 256 | bytes 2048 | tf_op jit(solution)/shard_map/psum | solution.py:208
  53.2 5.1 %all-gather.5.cloned.1.call-done = bf16[640,2048]{1,0:T(8,128)(2,1)} async-done(((bf16[160,2048]{1,0:T(8,128)(2,1)}), bf16[640,2048]{1,0:T(8,128)(2,1)}) %all-gather.5.cloned.1.call-update) | async-done | bytes 2621456 | tf_op jit(solution)/shard_map/all_gather | solution.py:189
  60.6 8.1 %all-to-all-start = ((bf16[32,8,768]{2,1,0:T(8,128)(2,1)}), bf16[32,8,768]{2,1,0:T(8,128)(2,1)}, u32[]{:S(2)}, u32[]{:S(2)}) async-start(bf16[32,8,768]{2,1,0:T(8,128)(2,1)} %broadcast_in_dim.97), calls=%async_computation | async-start | bytes 786432 | tf_op jit(solution)/shard_map/all_to_all | solution.py:162
  71.3 4.3 %collective-permute-start.5 = (bf16[352,2048]{1,0:T(8,128)(2,1)S(1)}, bf16[352,2048]{1,0:T(8,128)(2,1)}, u32[]{:S(2)}, u32[]{:S(2)}) collective-permute-start(bf16[352,2048]{1,0:T(8,128)(2,1)S(1)} %pad.9.refs_3_), channel_id=1, source_target_pairs={{1,0},{2,1},{3,2},{0,3},{5,4},{6,5},{7,6},{4,7},{9,8},{10,9},{11,1... | collective-permute-start | bytes 4325384 | tf_op jit(solution)/shard_map/ppermute | solution.py:17
  75.5 7.1 %all-to-all-done = bf16[32,8,768]{2,1,0:T(8,128)(2,1)} async-done(((bf16[32,8,768]{2,1,0:T(8,128)(2,1)}), bf16[32,8,768]{2,1,0:T(8,128)(2,1)}, u32[]{:S(2)}, u32[]{:S(2)}) %all-to-all-start) | async-done | bytes 393248 | tf_op jit(solution)/shard_map/all_to_all | solution.py:162
  83.9 7.4 %collective-permute-start.2 = (bf16[256,256]{1,0:T(8,128)(2,1)S(1)}, bf16[256,256]{1,0:T(8,128)(2,1)S(1)}, u32[]{:S(2)}, u32[]{:S(2)}) collective-permute-start(bf16[256,256]{1,0:T(8,128)(2,1)S(1)} %get-tuple-element.92), channel_id=1, source_target_pairs={{0,128},{128,0},{256,384},{384,256},{1,129},{129,1},{257,385},{385... | collective-permute-start | bytes 393224 | tf_op jit(solution)/shard_map/ppermute | solution.py:157
  91.3 12.0 %collective-permute-done.2 = bf16[256,256]{1,0:T(8,128)(2,1)S(1)} collective-permute-done((bf16[256,256]{1,0:T(8,128)(2,1)S(1)}, bf16[256,256]{1,0:T(8,128)(2,1)S(1)}, u32[]{:S(2)}, u32[]{:S(2)}) %collective-permute-start.2) | collective-permute-done | bytes 131104 | tf_op jit(solution)/shard_map/ppermute | solution.py:157
  106.5 8.8 %collective-permute-done.3 = bf16[256,256]{1,0:T(8,128)(2,1)S(1)} collective-permute-done((bf16[256,256]{1,0:T(8,128)(2,1)S(1)}, bf16[256,256]{1,0:T(8,128)(2,1)S(1)}, u32[]{:S(2)}, u32[]{:S(2)}) %collective-permute-start.3) | collective-permute-done | bytes 131104 | tf_op jit(solution)/shard_map/ppermute | solution.py:157
  115.5 24.3 %all_to_all.25.refs_1_ = bf16[4,256,256]{2,1,0:T(8,128)(2,1)} all-to-all(bf16[4,256,256]{2,1,0:T(8,128)(2,1)S(1)} %broadcast_in_dim.98), channel_id=1, replica_groups=mesh['section'=4,'zl'=4,'y'=4,'core'=2,'dp'=4] {'zl'}, dimensions={0} | all-to-all | bytes 1048576 | tf_op jit(solution)/shard_map/all_to_all | solution.py:162
  139.7 5.3 %all-gather.7.cloned.1.call-done = bf16[8192,256]{1,0:T(8,128)(2,1)} async-done(((bf16[256,256]{1,0:T(8,128)(2,1)}), bf16[8192,256]{1,0:T(8,128)(2,1)}) %all-gather.7.cloned.1.call-update) | async-done | bytes 4194320 | tf_op jit(solution)/shard_map/all_gather | solution.py:221
  147.7 4.5 %all-to-all-start.3 = ((bf16[4,4,256,256]{3,2,1,0:T(8,128)(2,1)}), bf16[4,4,256,256]{3,2,1,0:T(8,128)(2,1)}, u32[]{:S(2)}, u32[]{:S(2)}) async-start(bf16[4,4,256,256]{3,2,1,0:T(8,128)(2,1)} %broadcast_in_dim.101), calls=%async_computation.3 | async-start | bytes 4194304 | tf_op jit(solution)/shard_map/all_to_all | solution.py:162
  155.5 4.4 %collective-permute-start.7 = (bf16[176,2048]{1,0:T(8,128)(2,1)S(1)}, bf16[176,2048]{1,0:T(8,128)(2,1)S(1)}, u32[]{:S(2)}, u32[]{:S(2)}) collective-permute-start(bf16[176,2048]{1,0:T(8,128)(2,1)S(1)} %slice.461), channel_id=1, source_target_pairs={{1,0},{2,1},{3,2},{0,3},{5,4},{6,5},{7,6},{4,7},{9,8},{10,9},{11,1... | collective-permute-start | bytes 2162696 | tf_op jit(solution)/shard_map/ppermute | solution.py:17
  159.9 13.0 %collective-permute-done.6.refs_6_ = bf16[176,2048]{1,0:T(8,128)(2,1)S(1)} collective-permute-done((bf16[176,2048]{1,0:T(8,128)(2,1)S(1)}, bf16[176,2048]{1,0:T(8,128)(2,1)S(1)}, u32[]{:S(2)}, u32[]{:S(2)}) %collective-permute-start.6) | collective-permute-done | bytes 720928 | tf_op jit(solution)/shard_map/ppermute | solution.py:17
  178.4 3.1 %collective-permute-start.8 = (bf16[4,4,256,256]{3,2,1,0:T(8,128)(2,1)}, bf16[4,4,256,256]{3,2,1,0:T(8,128)(2,1)}, u32[]{:S(2)}, u32[]{:S(2)}) collective-permute-start(bf16[4,4,256,256]{3,2,1,0:T(8,128)(2,1)} %all-to-all-done.3.refs_0_), channel_id=1, source_target_pairs={{0,4},{4,0},{1,5},{5,1},{2,6},{6,2},{3,7},{7,3},{8,12},{12,8},{9,1... | collective-permute-start | bytes 6291464 | tf_op jit(solution)/shard_map/ppermute | solution.py:245
  184.3 9.1 %shard_map.122 = f32[8,512]{1,0:T(8,128)} custom-call(s32[2]{0:T(128)} %pad_add_fusion.2.own_ref, f32[32,1,256]{2,1,0:T(1,128)} %bitcast.81, s32[256,2]{1,0:T(8,128)} %copy.38.meta_ref, bf16[4,4,2,256,256]{4,3,2,1,0:T(8,128)(2,1)} %bitcast.74, bf16[4,256,256]{2,1,0:T(8,128)(2,1)} %all_to_all.25.refs_1_, bf16[4,160,2048]{2,1,0:T(8,128)(2,1)} %bitcast.72, ...), custom_call_target="tpu_custom_call" | custom-call | flops 2147483648 | bytes 12582912 | tf_op jit(solution)/shard_map/pallas_call | solution.py:130
  193.5 8.3 %shard_map.123 = f32[8,512]{1,0:T(8,128)} custom-call(s32[2]{0:T(128)} %pad_add_fusion.2.own_ref, f32[32,1,256]{2,1,0:T(1,128)} %bitcast.82, s32[256,2]{1,0:T(8,128)} %copy.39.meta_ref, bf16[4,4,256,256]{3,2,1,0:T(8,128)(2,1)} %all-to-all-done.3.refs_0_, bf16[4,4,256,256]{3,2,1,0:T(8,128)(2,1)} %collective-permute-done.8.refs_1_, ...), custom_call_target="tpu_custom_call" | custom-call | flops 2147483648 | bytes 12582912 | tf_op jit(solution)/shard_map/pallas_call | solution.py:130
  202.5 9.4 %collective-permute-start.9 = (f32[3,512]{1,0:T(4,128)S(1)}, f32[3,512]{1,0:T(4,128)S(1)}, u32[]{:S(2)}, u32[]{:S(2)}) collective-permute-start(f32[3,512]{1,0:T(4,128)S(1)} %slice_add_fusion), channel_id=1, source_target_pairs={{0,128},{128,0},{256,384},{384,256},{1,129},{129,1},{257,385},{385... | collective-permute-start | bytes 18440 | tf_op jit(solution)/shard_map/ppermute | solution.py:157
  213.1 7.3 %collective-permute-start.10 = (f32[3,512]{1,0:T(4,128)S(1)}, f32[3,512]{1,0:T(4,128)S(1)}, u32[]{:S(2)}, u32[]{:S(2)}) collective-permute-start(f32[3,512]{1,0:T(4,128)S(1)} %get-tuple-element.91), channel_id=1, source_target_pairs={{0,384},{128,256},{256,128},{384,0},{1,385},{129,257},{257,129},{3... | collective-permute-start | bytes 18440 | tf_op jit(solution)/shard_map/ppermute | solution.py:157
  222.2 6.3 %all-to-all-start.4 = ((f32[32,3,128]{2,1,0:T(4,128)}), f32[32,3,128]{2,1,0:T(4,128)S(1)}, u32[]{:S(2)}, u32[]{:S(2)}) async-start(f32[32,3,128]{2,1,0:T(4,128)} %broadcast_in_dim.104), calls=%async_computation.4 | async-start | bytes 131072 | tf_op jit(solution)/shard_map/all_to_all | solution.py:162
  229.2 7.1 %all-to-all-done.4 = f32[32,3,128]{2,1,0:T(4,128)S(1)} async-done(((f32[32,3,128]{2,1,0:T(4,128)}), f32[32,3,128]{2,1,0:T(4,128)S(1)}, u32[]{:S(2)}, u32[]{:S(2)}) %all-to-all-start.4) | async-done | bytes 49184 | tf_op jit(solution)/shard_map/all_to_all | solution.py:162
  (102 shorter events, 32.2 us)
Async XLA Ops:
  7.2 75.5 %copy-start = (bf16[768,256]{1,0:T(8,128)(2,1)S(1)}, bf16[768,256]{1,0:T(8,128)(2,1)}, u32[]{:S(2)}) copy-start(bf16[768,256]{1,0:T(8,128)(2,1)} %param.16) | copy-start | bytes 1179652
  7.2 51.1 %all-gather.5.cloned.1.call-start = ((), (), s32[]{:S(2)}) async-start(), calls=%async_computation.5 | async-start | bytes 3276800 | tf_op jit(solution)/shard_map/all_gather | solution.py:189
  9.4 23.0 %collective-permute-start = (bf16[3,32,768]{2,1,0:T(8,128)(2,1)S(1)}, bf16[3,32,768]{2,1,0:T(8,128)(2,1)S(1)}, u32[]{:S(2)}, u32[]{:S(2)}) collective-permute-start(bf16[3,32,768]{2,1,0:T(8,128)(2,1)S(1)} %get-tuple-element.82), channel_id=1, source_target_pairs={{0,4},{4,8},{8,12},{12,16},{16,20},{20,24},{24,28},{28,32},{32,36}... | collective-permute-start | bytes 442376 | tf_op jit(solution)/shard_map/ppermute | solution.py:26
  14.1 18.2 %collective-permute-start.1 = (bf16[3,32,768]{2,1,0:T(8,128)(2,1)S(1)}, bf16[3,32,768]{2,1,0:T(8,128)(2,1)S(1)}, u32[]{:S(2)}, u32[]{:S(2)}) collective-permute-start(bf16[3,32,768]{2,1,0:T(8,128)(2,1)S(1)} %get-tuple-element.83), channel_id=1, source_target_pairs={{4,0},{8,4},{12,8},{16,12},{20,16},{24,20},{28,24},{32,28},{36,32}... | collective-permute-start | bytes 442376 | tf_op jit(solution)/shard_map/ppermute | solution.py:28
  20.3 32.8 %all-to-all-start.2 = ((bf16[4,128,256]{2,1,0:T(8,128)(2,1)}), bf16[4,128,256]{2,1,0:T(8,128)(2,1)S(1)}, u32[]{:S(2)}, u32[]{:S(2)}) async-start(bf16[4,128,256]{2,1,0:T(8,128)(2,1)} %broadcast_in_dim.100), calls=%async_computation.2 | async-start | bytes 524288 | tf_op jit(solution)/shard_map/all_to_all | solution.py:162
  31.6 113.5 %all-gather.7.cloned.1.call-start = ((), (), s32[]{:S(2)}) async-start(), calls=%async_computation.6 | async-start | bytes 4325376 | tf_op jit(solution)/shard_map/all_gather | solution.py:221
  32.5 26.9 %copy-start.10 = (f32[768]{0:T(1024)S(1)}, f32[768]{0:T(1024)}, u32[]{:S(2)}) copy-start(f32[768]{0:T(1024)} %param.14) | copy-start | bytes 9220
  32.5 26.9 %copy-start.11 = (f32[768]{0:T(1024)S(1)}, f32[768]{0:T(1024)}, u32[]{:S(2)}) copy-start(f32[768]{0:T(1024)} %param.13) | copy-start | bytes 9220
  32.5 26.9 %copy-start.12 = (f32[768]{0:T(1024)S(1)}, f32[768]{0:T(1024)}, u32[]{:S(2)}) copy-start(f32[768]{0:T(1024)} %param.15) | copy-start | bytes 9220
  60.6 22.1 %all-to-all-start = ((bf16[32,8,768]{2,1,0:T(8,128)(2,1)}), bf16[32,8,768]{2,1,0:T(8,128)(2,1)}, u32[]{:S(2)}, u32[]{:S(2)}) async-start(bf16[32,8,768]{2,1,0:T(8,128)(2,1)} %broadcast_in_dim.97), calls=%async_computation | async-start | bytes 786432 | tf_op jit(solution)/shard_map/all_to_all | solution.py:162
  69.0 46.4 %copy-start.1 = (bf16[352,2048]{1,0:T(8,128)(2,1)}, bf16[352,2048]{1,0:T(8,128)(2,1)S(1)}, u32[]{:S(2)}) copy-start(bf16[352,2048]{1,0:T(8,128)(2,1)S(1)} %pad.9.refs_3_) | copy-start | bytes 4325380
  69.0 46.4 %collective-permute-start.4 = (bf16[352,2048]{1,0:T(8,128)(2,1)S(1)}, bf16[352,2048]{1,0:T(8,128)(2,1)S(1)}, u32[]{:S(2)}, u32[]{:S(2)}) collective-permute-start(bf16[352,2048]{1,0:T(8,128)(2,1)S(1)} %pad.9.refs_3_), channel_id=1, source_target_pairs={{3,0},{0,1},{1,2},{2,3},{7,4},{4,5},{5,6},{6,7},{11,8},{8,9},{9,10... | collective-permute-start | bytes 4325384 | tf_op jit(solution)/shard_map/ppermute | solution.py:17
  71.3 44.1 %collective-permute-start.5 = (bf16[352,2048]{1,0:T(8,128)(2,1)S(1)}, bf16[352,2048]{1,0:T(8,128)(2,1)}, u32[]{:S(2)}, u32[]{:S(2)}) collective-permute-start(bf16[352,2048]{1,0:T(8,128)(2,1)S(1)} %pad.9.refs_3_), channel_id=1, source_target_pairs={{1,0},{2,1},{3,2},{0,3},{5,4},{6,5},{7,6},{4,7},{9,8},{10,9},{11,1... | collective-permute-start | bytes 4325384 | tf_op jit(solution)/shard_map/ppermute | solution.py:17
  83.9 19.4 %collective-permute-start.2 = (bf16[256,256]{1,0:T(8,128)(2,1)S(1)}, bf16[256,256]{1,0:T(8,128)(2,1)S(1)}, u32[]{:S(2)}, u32[]{:S(2)}) collective-permute-start(bf16[256,256]{1,0:T(8,128)(2,1)S(1)} %get-tuple-element.92), channel_id=1, source_target_pairs={{0,128},{128,0},{256,384},{384,256},{1,129},{129,1},{257,385},{385... | collective-permute-start | bytes 393224 | tf_op jit(solution)/shard_map/ppermute | solution.py:157
  103.4 12.0 %collective-permute-start.3 = (bf16[256,256]{1,0:T(8,128)(2,1)S(1)}, bf16[256,256]{1,0:T(8,128)(2,1)S(1)}, u32[]{:S(2)}, u32[]{:S(2)}) collective-permute-start(bf16[256,256]{1,0:T(8,128)(2,1)S(1)} %fusion.63), channel_id=1, source_target_pairs={{0,384},{128,256},{256,128},{384,0},{1,385},{129,257},{257,129},{3... | collective-permute-start | bytes 393224 | tf_op jit(solution)/shard_map/ppermute | solution.py:157
  115.4 36.8 %copy-start.2 = (bf16[352,2048]{1,0:T(8,128)(2,1)}, bf16[352,2048]{1,0:T(8,128)(2,1)S(1)}, u32[]{:S(2)}) copy-start(bf16[352,2048]{1,0:T(8,128)(2,1)S(1)} %collective-permute-done.4.refs_4_) | copy-start | bytes 4325380
  147.7 30.8 %all-to-all-start.3 = ((bf16[4,4,256,256]{3,2,1,0:T(8,128)(2,1)}), bf16[4,4,256,256]{3,2,1,0:T(8,128)(2,1)}, u32[]{:S(2)}, u32[]{:S(2)}) async-start(bf16[4,4,256,256]{3,2,1,0:T(8,128)(2,1)} %broadcast_in_dim.101), calls=%async_computation.3 | async-start | bytes 4194304 | tf_op jit(solution)/shard_map/all_to_all | solution.py:162
  152.2 29.6 %copy-start.14 = (s32[1,512]{1,0:T(1,128)S(1)}, s32[1,512]{1,0:T(1,128)}, u32[]{:S(2)}) copy-start(s32[1,512]{1,0:T(1,128)} %param.21) | copy-start | bytes 6148
  152.2 20.7 %collective-permute-start.6 = (bf16[176,2048]{1,0:T(8,128)(2,1)S(1)}, bf16[176,2048]{1,0:T(8,128)(2,1)S(1)}, u32[]{:S(2)}, u32[]{:S(2)}) collective-permute-start(bf16[176,2048]{1,0:T(8,128)(2,1)S(1)} %slice.460), channel_id=1, source_target_pairs={{3,0},{0,1},{1,2},{2,3},{7,4},{4,5},{5,6},{6,7},{11,8},{8,9},{9,10... | collective-permute-start | bytes 2162696 | tf_op jit(solution)/shard_map/ppermute | solution.py:17
  155.5 20.5 %collective-permute-start.7 = (bf16[176,2048]{1,0:T(8,128)(2,1)S(1)}, bf16[176,2048]{1,0:T(8,128)(2,1)S(1)}, u32[]{:S(2)}, u32[]{:S(2)}) collective-permute-start(bf16[176,2048]{1,0:T(8,128)(2,1)S(1)} %slice.461), channel_id=1, source_target_pairs={{1,0},{2,1},{3,2},{0,3},{5,4},{6,5},{7,6},{4,7},{9,8},{10,9},{11,1... | collective-permute-start | bytes 2162696 | tf_op jit(solution)/shard_map/ppermute | solution.py:17
  178.4 15.1 %collective-permute-start.8 = (bf16[4,4,256,256]{3,2,1,0:T(8,128)(2,1)}, bf16[4,4,256,256]{3,2,1,0:T(8,128)(2,1)}, u32[]{:S(2)}, u32[]{:S(2)}) collective-permute-start(bf16[4,4,256,256]{3,2,1,0:T(8,128)(2,1)} %all-to-all-done.3.refs_0_), channel_id=1, source_target_pairs={{0,4},{4,0},{1,5},{5,1},{2,6},{6,2},{3,7},{7,3},{8,12},{12,8},{9,1... | collective-permute-start | bytes 6291464 | tf_op jit(solution)/shard_map/ppermute | solution.py:245
  202.5 10.5 %collective-permute-start.9 = (f32[3,512]{1,0:T(4,128)S(1)}, f32[3,512]{1,0:T(4,128)S(1)}, u32[]{:S(2)}, u32[]{:S(2)}) collective-permute-start(f32[3,512]{1,0:T(4,128)S(1)} %slice_add_fusion), channel_id=1, source_target_pairs={{0,128},{128,0},{256,384},{384,256},{1,129},{129,1},{257,385},{385... | collective-permute-start | bytes 18440 | tf_op jit(solution)/shard_map/ppermute | solution.py:157
  213.1 8.4 %collective-permute-start.10 = (f32[3,512]{1,0:T(4,128)S(1)}, f32[3,512]{1,0:T(4,128)S(1)}, u32[]{:S(2)}, u32[]{:S(2)}) collective-permute-start(f32[3,512]{1,0:T(4,128)S(1)} %get-tuple-element.91), channel_id=1, source_target_pairs={{0,384},{128,256},{256,128},{384,0},{1,385},{129,257},{257,129},{3... | collective-permute-start | bytes 18440 | tf_op jit(solution)/shard_map/ppermute | solution.py:157
  222.2 14.1 %all-to-all-start.4 = ((f32[32,3,128]{2,1,0:T(4,128)}), f32[32,3,128]{2,1,0:T(4,128)S(1)}, u32[]{:S(2)}, u32[]{:S(2)}) async-start(f32[32,3,128]{2,1,0:T(4,128)} %broadcast_in_dim.104), calls=%async_computation.4 | async-start | bytes 131072 | tf_op jit(solution)/shard_map/all_to_all | solution.py:162
  (8 other events, 97.1 us)
Sparse Core Ops, SparseCore 0:
  10.1 48.1 all-gather.4
  60.4 84.5 all-gather.6
where the time goes:
time: 245 us; the launch traced here: 244 us
  starting transfers between devices  83.8 us (34%)
  waiting for transfers between devices  66.2 us (27%)
  blocking collectives  40.4 us (16%)
  Pallas kernels  17.4 us (7%)
  between operations  14.6 us (6%)
  local copies, waits for them, and re-layouts  10.9 us (4%)
  other arithmetic  8.33 us (3%)
    all_to_all x4, starting transfers between devices, to_all(): lax.all_to_all(jnp.broadcast_to(value[None], (count,) + value.shape), axi...  30.2 us
    ppermute x4, starting transfers between devices, across(): return lax.ppermute(value, 'section', pairs)  27.3 us
    all_to_all x1, blocking collectives, to_all(): lax.all_to_all(jnp.broadcast_to(value[None], (count,) + value.shape), axi...  24.3 us
    ppermute x4, waiting for transfers between devices, across(): return lax.ppermute(value, 'section', pairs)  23 us
    pallas_call x2, Pallas kernels, head_stats(): pl.pallas_call(functools.partial(head_kernel, columns, offsets, from_text...  17.4 us
    all_to_all x4, waiting for transfers between devices, to_all(): lax.all_to_all(jnp.broadcast_to(value[None], (count,) + value.shape), axi...  16.7 us
    psum x1, blocking collectives, shards(): sums = lax.psum(sums, 'section')  16.1 us
    ppermute x4, waiting for transfers between devices, shifted(): lax.ppermute(value, axis, [((i + step) % count, i) for i in range(count)])  16.1 us
  transfers between devices with their start and end apart: 17, of which 11 were waited for; matrix products, arithmetic and copies ran while one was open for 6% of the time, Pallas kernels for 4%

commit v1 on v0

--- a/solution.py
+++ b/solution.py
@@ -8,7 +8,7 @@
 from jax.sharding import PartitionSpec as P
 
 WIDE = 256
-LOW = 160
+LOW = 128
 VOCAB = ("zl", "y", "core")
 
 

time: 245 us -> 240 us (0.980)
  waiting for transfers between devices: 66.2 us -> 61.1 us
    all_gather x1, waiting for transfers between devices: 5.14 us -> 0.9 us  [shards(): low_all = lax.all_gather(weight[:LOW], 'dp', axis=0)]
    all_to_all x4, waiting for transfers between devices: 16.7 us -> 14.1 us  [to_all(): lax.all_to_all(jnp.broadcast_to(value[None], (count,) + value.shape), axi...]
  transfers between devices with their start and end apart: 17 -> 17, of which waited for: 11 -> 10; matrix products, arithmetic and copies ran while one was open for 6% -> 6% of each run, Pallas kernels for 4% -> 4%
where the time goes in v1:
time: 240 us; the launch traced here: 239 us
  starting transfers between devices  85.7 us (36%)
  waiting for transfers between devices  61.1 us (25%)
  blocking collectives  39.3 us (16%)
  Pallas kernels  17.4 us (7%)
  between operations  14.6 us (6%)
  local copies, waits for them, and re-layouts  10.9 us (5%)
  other arithmetic  8.29 us (3%)
    all_to_all x4, starting transfers between devices, to_all(): lax.all_to_all(jnp.broadcast_to(value[None], (count,) + value.shape), axi...  31.3 us
    ppermute x4, starting transfers between devices, across(): return lax.ppermute(value, 'section', pairs)  26.3 us
    ppermute x4, waiting for transfers between devices, across(): return lax.ppermute(value, 'section', pairs)  24.1 us
    all_to_all x1, blocking collectives, to_all(): lax.all_to_all(jnp.broadcast_to(value[None], (count,) + value.shape), axi...  23.2 us
    pallas_call x2, Pallas kernels, head_stats(): pl.pallas_call(functools.partial(head_kernel, columns, offsets, from_text...  17.4 us
    ppermute x4, waiting for transfers between devices, shifted(): lax.ppermute(value, axis, [((i + step) % count, i) for i in range(count)])  16.9 us
    psum x1, blocking collectives, shards(): sums = lax.psum(sums, 'section')  16.1 us
    ppermute x4, starting transfers between devices, shifted(): lax.ppermute(value, axis, [((i + step) % count, i) for i in range(count)])  14.7 us
  transfers between devices with their start and end apart: 17, of which 10 were waited for; matrix products, arithmetic and copies ran while one was open for 6% of the time, Pallas kernels for 4%

profile of v1, /device:TPU:1, one launch (start us, length us, event | category | flops | bytes accessed | tf_op | source)
XLA Modules:
  0.0 239.4 jit_solution(17097912709153297446)
XLA Ops:
  9.3 4.7 %collective-permute-start = (bf16[3,32,768]{2,1,0:T(8,128)(2,1)S(1)}, bf16[3,32,768]{2,1,0:T(8,128)(2,1)S(1)}, u32[]{:S(2)}, u32[]{:S(2)}) collective-permute-start(bf16[3,32,768]{2,1,0:T(8,128)(2,1)S(1)} %get-tuple-element.82), channel_id=1, source_target_pairs={{0,4},{4,8},{8,12},{12,16},{16,20},{20,24},{24,28},{28,32},{32,36}... | collective-permute-start | bytes 442376 | tf_op jit(solution)/shard_map/ppermute | solution.py:26
  14.0 5.5 %collective-permute-start.1 = (bf16[3,32,768]{2,1,0:T(8,128)(2,1)S(1)}, bf16[3,32,768]{2,1,0:T(8,128)(2,1)S(1)}, u32[]{:S(2)}, u32[]{:S(2)}) collective-permute-start(bf16[3,32,768]{2,1,0:T(8,128)(2,1)S(1)} %get-tuple-element.83), channel_id=1, source_target_pairs={{4,0},{8,4},{12,8},{16,12},{20,16},{24,20},{28,24},{32,28},{36,32}... | collective-permute-start | bytes 442376 | tf_op jit(solution)/shard_map/ppermute | solution.py:28
  20.2 11.2 %all-to-all-start.2 = ((bf16[4,128,256]{2,1,0:T(8,128)(2,1)}), bf16[4,128,256]{2,1,0:T(8,128)(2,1)S(1)}, u32[]{:S(2)}, u32[]{:S(2)}) async-start(bf16[4,128,256]{2,1,0:T(8,128)(2,1)} %broadcast_in_dim.100), calls=%async_computation.2 | async-start | bytes 524288 | tf_op jit(solution)/shard_map/all_to_all | solution.py:162
  32.4 4.3 %fusion.79 = (f32[4,32]{1,0:T(4,128)S(1)}, f32[4,32]{1,0:T(4,128)S(1)}, f32[4,32,768]{2,1,0:T(8,128)S(1)}) fusion(f32[768]{0:T(1024)S(1)} %get-tuple-element.71, f32[10,38,768]{2,1,0:T(8,128)S(1)} %fusion.7, f32[768]{0:T(1024)S(1)} %get-tuple-element.72, f32[768]{0:T(1024)S(1)} %get-tuple-element.25, f32[768]{0:T(1024)S(1)} %get-tuple-element.26, ...), kind=kLoop, calls=%fused_computation.221 | loop fusion | flops 9830144 | bytes 19812352 | tf_op jit(solution)/shard_map/reduce_sum | solution.py:206
  36.9 16.1 %psum.7 = f32[2,128]{1,0:T(2,128)S(1)} all-reduce(f32[2,128]{1,0:T(2,128)S(1)} %pad_maximum_fusion.5), channel_id=1, replica_groups=mesh['section'=4,'zl'=4,'y'=4,'core'=2,'dp'=4] {'section'}, use_global_device_ids=true, to_apply=%region_2.3 | all-reduce | flops 256 | bytes 2048 | tf_op jit(solution)/shard_map/psum | solution.py:208
  56.2 9.0 %all-to-all-start = ((bf16[32,8,768]{2,1,0:T(8,128)(2,1)}), bf16[32,8,768]{2,1,0:T(8,128)(2,1)}, u32[]{:S(2)}, u32[]{:S(2)}) async-start(bf16[32,8,768]{2,1,0:T(8,128)(2,1)} %broadcast_in_dim.97), calls=%async_computation | async-start | bytes 786432 | tf_op jit(solution)/shard_map/all_to_all | solution.py:162
  68.8 3.4 %collective-permute-start.5 = (bf16[384,2048]{1,0:T(8,128)(2,1)S(1)}, bf16[384,2048]{1,0:T(8,128)(2,1)}, u32[]{:S(2)}, u32[]{:S(2)}) collective-permute-start(bf16[384,2048]{1,0:T(8,128)(2,1)S(1)} %pad.9.refs_3_), channel_id=1, source_target_pairs={{1,0},{2,1},{3,2},{0,3},{5,4},{6,5},{7,6},{4,7},{9,8},{10,9},{11,1... | collective-permute-start | bytes 4718600 | tf_op jit(solution)/shard_map/ppermute | solution.py:17
  72.2 6.9 %all-to-all-done = bf16[32,8,768]{2,1,0:T(8,128)(2,1)} async-done(((bf16[32,8,768]{2,1,0:T(8,128)(2,1)}), bf16[32,8,768]{2,1,0:T(8,128)(2,1)}, u32[]{:S(2)}, u32[]{:S(2)}) %all-to-all-start) | async-done | bytes 393248 | tf_op jit(solution)/shard_map/all_to_all | solution.py:162
  80.4 6.6 %collective-permute-start.2 = (bf16[256,256]{1,0:T(8,128)(2,1)S(1)}, bf16[256,256]{1,0:T(8,128)(2,1)S(1)}, u32[]{:S(2)}, u32[]{:S(2)}) collective-permute-start(bf16[256,256]{1,0:T(8,128)(2,1)S(1)} %get-tuple-element.92), channel_id=1, source_target_pairs={{0,128},{128,0},{256,384},{384,256},{1,129},{129,1},{257,385},{385... | collective-permute-start | bytes 393224 | tf_op jit(solution)/shard_map/ppermute | solution.py:157
  87.0 12.5 %collective-permute-done.2 = bf16[256,256]{1,0:T(8,128)(2,1)S(1)} collective-permute-done((bf16[256,256]{1,0:T(8,128)(2,1)S(1)}, bf16[256,256]{1,0:T(8,128)(2,1)S(1)}, u32[]{:S(2)}, u32[]{:S(2)}) %collective-permute-start.2) | collective-permute-done | bytes 131104 | tf_op jit(solution)/shard_map/ppermute | solution.py:157
  102.2 9.6 %collective-permute-done.3 = bf16[256,256]{1,0:T(8,128)(2,1)S(1)} collective-permute-done((bf16[256,256]{1,0:T(8,128)(2,1)S(1)}, bf16[256,256]{1,0:T(8,128)(2,1)S(1)}, u32[]{:S(2)}, u32[]{:S(2)}) %collective-permute-start.3) | collective-permute-done | bytes 131104 | tf_op jit(solution)/shard_map/ppermute | solution.py:157
  111.9 23.2 %all_to_all.25.refs_1_ = bf16[4,256,256]{2,1,0:T(8,128)(2,1)} all-to-all(bf16[4,256,256]{2,1,0:T(8,128)(2,1)S(1)} %broadcast_in_dim.98), channel_id=1, replica_groups=mesh['section'=4,'zl'=4,'y'=4,'core'=2,'dp'=4] {'zl'}, dimensions={0} | all-to-all | bytes 1048576 | tf_op jit(solution)/shard_map/all_to_all | solution.py:162
  135.1 5.1 %all-gather.7.cloned.1.call-done = bf16[8192,256]{1,0:T(8,128)(2,1)} async-done(((bf16[256,256]{1,0:T(8,128)(2,1)}), bf16[8192,256]{1,0:T(8,128)(2,1)}) %all-gather.7.cloned.1.call-update) | async-done | bytes 4194320 | tf_op jit(solution)/shard_map/all_gather | solution.py:221
  142.8 4.5 %all-to-all-start.3 = ((bf16[4,4,256,256]{3,2,1,0:T(8,128)(2,1)}), bf16[4,4,256,256]{3,2,1,0:T(8,128)(2,1)}, u32[]{:S(2)}, u32[]{:S(2)}) async-start(bf16[4,4,256,256]{3,2,1,0:T(8,128)(2,1)} %broadcast_in_dim.101), calls=%async_computation.3 | async-start | bytes 4194304 | tf_op jit(solution)/shard_map/all_to_all | solution.py:162
  147.3 4.3 %collective-permute-start.6 = (bf16[192,2048]{1,0:T(8,128)(2,1)S(1)}, bf16[192,2048]{1,0:T(8,128)(2,1)S(1)}, u32[]{:S(2)}, u32[]{:S(2)}) collective-permute-start(bf16[192,2048]{1,0:T(8,128)(2,1)S(1)} %slice.460), channel_id=1, source_target_pairs={{3,0},{0,1},{1,2},{2,3},{7,4},{4,5},{5,6},{6,7},{11,8},{8,9},{9,10... | collective-permute-start | bytes 2359304 | tf_op jit(solution)/shard_map/ppermute | solution.py:17
  152.9 3.8 %collective-permute-start.7 = (bf16[192,2048]{1,0:T(8,128)(2,1)S(1)}, bf16[192,2048]{1,0:T(8,128)(2,1)S(1)}, u32[]{:S(2)}, u32[]{:S(2)}) collective-permute-start(bf16[192,2048]{1,0:T(8,128)(2,1)S(1)} %slice.461), channel_id=1, source_target_pairs={{1,0},{2,1},{3,2},{0,3},{5,4},{6,5},{7,6},{4,7},{9,8},{10,9},{11,1... | collective-permute-start | bytes 2359304 | tf_op jit(solution)/shard_map/ppermute | solution.py:17
  156.7 14.7 %collective-permute-done.6.refs_6_ = bf16[192,2048]{1,0:T(8,128)(2,1)S(1)} collective-permute-done((bf16[192,2048]{1,0:T(8,128)(2,1)S(1)}, bf16[192,2048]{1,0:T(8,128)(2,1)S(1)}, u32[]{:S(2)}, u32[]{:S(2)}) %collective-permute-start.6) | collective-permute-done | bytes 786464 | tf_op jit(solution)/shard_map/ppermute | solution.py:17
  173.6 3.3 %collective-permute-start.8 = (bf16[4,4,256,256]{3,2,1,0:T(8,128)(2,1)}, bf16[4,4,256,256]{3,2,1,0:T(8,128)(2,1)}, u32[]{:S(2)}, u32[]{:S(2)}) collective-permute-start(bf16[4,4,256,256]{3,2,1,0:T(8,128)(2,1)} %all-to-all-done.3.refs_0_), channel_id=1, source_target_pairs={{0,4},{4,0},{1,5},{5,1},{2,6},{6,2},{3,7},{7,3},{8,12},{12,8},{9,1... | collective-permute-start | bytes 6291464 | tf_op jit(solution)/shard_map/ppermute | solution.py:245
  179.6 9.1 %shard_map.122 = f32[8,512]{1,0:T(8,128)} custom-call(s32[2]{0:T(128)} %pad_add_fusion.2.own_ref, f32[32,1,256]{2,1,0:T(1,128)} %bitcast.81, s32[256,2]{1,0:T(8,128)} %copy.38.meta_ref, bf16[4,4,2,256,256]{4,3,2,1,0:T(8,128)(2,1)} %bitcast.74, bf16[4,256,256]{2,1,0:T(8,128)(2,1)} %all_to_all.25.refs_1_, bf16[4,128,2048]{2,1,0:T(8,128)(2,1)} %bitcast.72, ...), custom_call_target="tpu_custom_call" | custom-call | flops 2147483648 | bytes 12582912 | tf_op jit(solution)/shard_map/pallas_call | solution.py:130
  188.8 8.3 %shard_map.123 = f32[8,512]{1,0:T(8,128)} custom-call(s32[2]{0:T(128)} %pad_add_fusion.2.own_ref, f32[32,1,256]{2,1,0:T(1,128)} %bitcast.82, s32[256,2]{1,0:T(8,128)} %copy.39.meta_ref, bf16[4,4,256,256]{3,2,1,0:T(8,128)(2,1)} %all-to-all-done.3.refs_0_, bf16[4,4,256,256]{3,2,1,0:T(8,128)(2,1)} %collective-permute-done.8.refs_1_, ...), custom_call_target="tpu_custom_call" | custom-call | flops 2147483648 | bytes 12582912 | tf_op jit(solution)/shard_map/pallas_call | solution.py:130
  197.8 8.1 %collective-permute-start.9 = (f32[3,512]{1,0:T(4,128)S(1)}, f32[3,512]{1,0:T(4,128)S(1)}, u32[]{:S(2)}, u32[]{:S(2)}) collective-permute-start(f32[3,512]{1,0:T(4,128)S(1)} %slice_add_fusion), channel_id=1, source_target_pairs={{0,128},{128,0},{256,384},{384,256},{1,129},{129,1},{257,385},{385... | collective-permute-start | bytes 18440 | tf_op jit(solution)/shard_map/ppermute | solution.py:157
  207.0 8.9 %collective-permute-start.10 = (f32[3,512]{1,0:T(4,128)S(1)}, f32[3,512]{1,0:T(4,128)S(1)}, u32[]{:S(2)}, u32[]{:S(2)}) collective-permute-start(f32[3,512]{1,0:T(4,128)S(1)} %get-tuple-element.91), channel_id=1, source_target_pairs={{0,384},{128,256},{256,128},{384,0},{1,385},{129,257},{257,129},{3... | collective-permute-start | bytes 18440 | tf_op jit(solution)/shard_map/ppermute | solution.py:157
  217.7 6.5 %all-to-all-start.4 = ((f32[32,3,128]{2,1,0:T(4,128)}), f32[32,3,128]{2,1,0:T(4,128)S(1)}, u32[]{:S(2)}, u32[]{:S(2)}) async-start(f32[32,3,128]{2,1,0:T(4,128)} %broadcast_in_dim.104), calls=%async_computation.4 | async-start | bytes 131072 | tf_op jit(solution)/shard_map/all_to_all | solution.py:162
  224.8 7.1 %all-to-all-done.4 = f32[32,3,128]{2,1,0:T(4,128)S(1)} async-done(((f32[32,3,128]{2,1,0:T(4,128)}), f32[32,3,128]{2,1,0:T(4,128)S(1)}, u32[]{:S(2)}, u32[]{:S(2)}) %all-to-all-start.4) | async-done | bytes 49184 | tf_op jit(solution)/shard_map/all_to_all | solution.py:162
  (106 shorter events, 28.1 us)
Async XLA Ops:
  7.2 72.0 %copy-start = (bf16[768,256]{1,0:T(8,128)(2,1)S(1)}, bf16[768,256]{1,0:T(8,128)(2,1)}, u32[]{:S(2)}) copy-start(bf16[768,256]{1,0:T(8,128)(2,1)} %param.16) | copy-start | bytes 1179652
  7.2 46.8 %all-gather.5.cloned.1.call-start = ((), (), s32[]{:S(2)}) async-start(), calls=%async_computation.5 | async-start | bytes 2621440 | tf_op jit(solution)/shard_map/all_gather | solution.py:189
  9.2 22.7 %copy-start.15 = (s32[1,256]{1,0:T(1,128)S(1)}, s32[1,256]{1,0:T(1,128)}, u32[]{:S(2)}) copy-start(s32[1,256]{1,0:T(1,128)} %param.18) | copy-start | bytes 3076
  9.3 23.0 %collective-permute-start = (bf16[3,32,768]{2,1,0:T(8,128)(2,1)S(1)}, bf16[3,32,768]{2,1,0:T(8,128)(2,1)S(1)}, u32[]{:S(2)}, u32[]{:S(2)}) collective-permute-start(bf16[3,32,768]{2,1,0:T(8,128)(2,1)S(1)} %get-tuple-element.82), channel_id=1, source_target_pairs={{0,4},{4,8},{8,12},{12,16},{16,20},{20,24},{24,28},{28,32},{32,36}... | collective-permute-start | bytes 442376 | tf_op jit(solution)/shard_map/ppermute | solution.py:26
  14.0 18.2 %collective-permute-start.1 = (bf16[3,32,768]{2,1,0:T(8,128)(2,1)S(1)}, bf16[3,32,768]{2,1,0:T(8,128)(2,1)S(1)}, u32[]{:S(2)}, u32[]{:S(2)}) collective-permute-start(bf16[3,32,768]{2,1,0:T(8,128)(2,1)S(1)} %get-tuple-element.83), channel_id=1, source_target_pairs={{4,0},{8,4},{12,8},{16,12},{20,16},{24,20},{28,24},{32,28},{36,32}... | collective-permute-start | bytes 442376 | tf_op jit(solution)/shard_map/ppermute | solution.py:28
  20.2 32.8 %all-to-all-start.2 = ((bf16[4,128,256]{2,1,0:T(8,128)(2,1)}), bf16[4,128,256]{2,1,0:T(8,128)(2,1)S(1)}, u32[]{:S(2)}, u32[]{:S(2)}) async-start(bf16[4,128,256]{2,1,0:T(8,128)(2,1)} %broadcast_in_dim.100), calls=%async_computation.2 | async-start | bytes 524288 | tf_op jit(solution)/shard_map/all_to_all | solution.py:162
  31.5 108.7 %all-gather.7.cloned.1.call-start = ((), (), s32[]{:S(2)}) async-start(), calls=%async_computation.6 | async-start | bytes 4325376 | tf_op jit(solution)/shard_map/all_gather | solution.py:221
  32.4 22.7 %copy-start.12 = (f32[768]{0:T(1024)S(1)}, f32[768]{0:T(1024)}, u32[]{:S(2)}) copy-start(f32[768]{0:T(1024)} %param.14) | copy-start | bytes 9220
  56.2 22.9 %all-to-all-start = ((bf16[32,8,768]{2,1,0:T(8,128)(2,1)}), bf16[32,8,768]{2,1,0:T(8,128)(2,1)}, u32[]{:S(2)}, u32[]{:S(2)}) async-start(bf16[32,8,768]{2,1,0:T(8,128)(2,1)} %broadcast_in_dim.97), calls=%async_computation | async-start | bytes 786432 | tf_op jit(solution)/shard_map/all_to_all | solution.py:162
  65.7 46.2 %copy-start.1 = (bf16[384,2048]{1,0:T(8,128)(2,1)}, bf16[384,2048]{1,0:T(8,128)(2,1)S(1)}, u32[]{:S(2)}) copy-start(bf16[384,2048]{1,0:T(8,128)(2,1)S(1)} %pad.9.refs_3_) | copy-start | bytes 4718596
  65.7 46.1 %collective-permute-start.4 = (bf16[384,2048]{1,0:T(8,128)(2,1)S(1)}, bf16[384,2048]{1,0:T(8,128)(2,1)S(1)}, u32[]{:S(2)}, u32[]{:S(2)}) collective-permute-start(bf16[384,2048]{1,0:T(8,128)(2,1)S(1)} %pad.9.refs_3_), channel_id=1, source_target_pairs={{3,0},{0,1},{1,2},{2,3},{7,4},{4,5},{5,6},{6,7},{11,8},{8,9},{9,10... | collective-permute-start | bytes 4718600 | tf_op jit(solution)/shard_map/ppermute | solution.py:17
  68.8 43.0 %collective-permute-start.5 = (bf16[384,2048]{1,0:T(8,128)(2,1)S(1)}, bf16[384,2048]{1,0:T(8,128)(2,1)}, u32[]{:S(2)}, u32[]{:S(2)}) collective-permute-start(bf16[384,2048]{1,0:T(8,128)(2,1)S(1)} %pad.9.refs_3_), channel_id=1, source_target_pairs={{1,0},{2,1},{3,2},{0,3},{5,4},{6,5},{7,6},{4,7},{9,8},{10,9},{11,1... | collective-permute-start | bytes 4718600 | tf_op jit(solution)/shard_map/ppermute | solution.py:17
  80.4 19.1 %collective-permute-start.2 = (bf16[256,256]{1,0:T(8,128)(2,1)S(1)}, bf16[256,256]{1,0:T(8,128)(2,1)S(1)}, u32[]{:S(2)}, u32[]{:S(2)}) collective-permute-start(bf16[256,256]{1,0:T(8,128)(2,1)S(1)} %get-tuple-element.92), channel_id=1, source_target_pairs={{0,128},{128,0},{256,384},{384,256},{1,129},{129,1},{257,385},{385... | collective-permute-start | bytes 393224 | tf_op jit(solution)/shard_map/ppermute | solution.py:157
  99.5 12.3 %collective-permute-start.3 = (bf16[256,256]{1,0:T(8,128)(2,1)S(1)}, bf16[256,256]{1,0:T(8,128)(2,1)S(1)}, u32[]{:S(2)}, u32[]{:S(2)}) collective-permute-start(bf16[256,256]{1,0:T(8,128)(2,1)S(1)} %fusion.63), channel_id=1, source_target_pairs={{0,384},{128,256},{256,128},{384,0},{1,385},{129,257},{257,129},{3... | collective-permute-start | bytes 393224 | tf_op jit(solution)/shard_map/ppermute | solution.py:157
  111.8 35.5 %copy-start.2 = (bf16[384,2048]{1,0:T(8,128)(2,1)}, bf16[384,2048]{1,0:T(8,128)(2,1)S(1)}, u32[]{:S(2)}) copy-start(bf16[384,2048]{1,0:T(8,128)(2,1)S(1)} %collective-permute-done.4.refs_4_) | copy-start | bytes 4718596
  142.8 30.9 %all-to-all-start.3 = ((bf16[4,4,256,256]{3,2,1,0:T(8,128)(2,1)}), bf16[4,4,256,256]{3,2,1,0:T(8,128)(2,1)}, u32[]{:S(2)}, u32[]{:S(2)}) async-start(bf16[4,4,256,256]{3,2,1,0:T(8,128)(2,1)} %broadcast_in_dim.101), calls=%async_computation.3 | async-start | bytes 4194304 | tf_op jit(solution)/shard_map/all_to_all | solution.py:162
  147.3 29.9 %copy-start.16 = (s32[1,512]{1,0:T(1,128)S(1)}, s32[1,512]{1,0:T(1,128)}, u32[]{:S(2)}) copy-start(s32[1,512]{1,0:T(1,128)} %param.21) | copy-start | bytes 6148
  147.3 24.1 %collective-permute-start.6 = (bf16[192,2048]{1,0:T(8,128)(2,1)S(1)}, bf16[192,2048]{1,0:T(8,128)(2,1)S(1)}, u32[]{:S(2)}, u32[]{:S(2)}) collective-permute-start(bf16[192,2048]{1,0:T(8,128)(2,1)S(1)} %slice.460), channel_id=1, source_target_pairs={{3,0},{0,1},{1,2},{2,3},{7,4},{4,5},{5,6},{6,7},{11,8},{8,9},{9,10... | collective-permute-start | bytes 2359304 | tf_op jit(solution)/shard_map/ppermute | solution.py:17
  152.9 20.7 %collective-permute-start.7 = (bf16[192,2048]{1,0:T(8,128)(2,1)S(1)}, bf16[192,2048]{1,0:T(8,128)(2,1)S(1)}, u32[]{:S(2)}, u32[]{:S(2)}) collective-permute-start(bf16[192,2048]{1,0:T(8,128)(2,1)S(1)} %slice.461), channel_id=1, source_target_pairs={{1,0},{2,1},{3,2},{0,3},{5,4},{6,5},{7,6},{4,7},{9,8},{10,9},{11,1... | collective-permute-start | bytes 2359304 | tf_op jit(solution)/shard_map/ppermute | solution.py:17
  173.6 15.1 %collective-permute-start.8 = (bf16[4,4,256,256]{3,2,1,0:T(8,128)(2,1)}, bf16[4,4,256,256]{3,2,1,0:T(8,128)(2,1)}, u32[]{:S(2)}, u32[]{:S(2)}) collective-permute-start(bf16[4,4,256,256]{3,2,1,0:T(8,128)(2,1)} %all-to-all-done.3.refs_0_), channel_id=1, source_target_pairs={{0,4},{4,0},{1,5},{5,1},{2,6},{6,2},{3,7},{7,3},{8,12},{12,8},{9,1... | collective-permute-start | bytes 6291464 | tf_op jit(solution)/shard_map/ppermute | solution.py:245
  188.7 35.5 %copy-start.8 = (f32[8,768]{1,0:T(8,128)S(1)}, f32[8,768]{1,0:T(8,128)}, u32[]{:S(2)}) copy-start(f32[8,768]{1,0:T(8,128)} %copy-done.7) | copy-start | bytes 73732
  197.8 9.2 %collective-permute-start.9 = (f32[3,512]{1,0:T(4,128)S(1)}, f32[3,512]{1,0:T(4,128)S(1)}, u32[]{:S(2)}, u32[]{:S(2)}) collective-permute-start(f32[3,512]{1,0:T(4,128)S(1)} %slice_add_fusion), channel_id=1, source_target_pairs={{0,128},{128,0},{256,384},{384,256},{1,129},{129,1},{257,385},{385... | collective-permute-start | bytes 18440 | tf_op jit(solution)/shard_map/ppermute | solution.py:157
  207.0 9.9 %collective-permute-start.10 = (f32[3,512]{1,0:T(4,128)S(1)}, f32[3,512]{1,0:T(4,128)S(1)}, u32[]{:S(2)}, u32[]{:S(2)}) collective-permute-start(f32[3,512]{1,0:T(4,128)S(1)} %get-tuple-element.91), channel_id=1, source_target_pairs={{0,384},{128,256},{256,128},{384,0},{1,385},{129,257},{257,129},{3... | collective-permute-start | bytes 18440 | tf_op jit(solution)/shard_map/ppermute | solution.py:157
  217.7 14.3 %all-to-all-start.4 = ((f32[32,3,128]{2,1,0:T(4,128)}), f32[32,3,128]{2,1,0:T(4,128)S(1)}, u32[]{:S(2)}, u32[]{:S(2)}) async-start(f32[32,3,128]{2,1,0:T(4,128)} %broadcast_in_dim.104), calls=%async_computation.4 | async-start | bytes 131072 | tf_op jit(solution)/shard_map/all_to_all | solution.py:162
  (10 other events, 124.9 us)
Sparse Core Ops, SparseCore 0:
  10.1 43.7 all-gather.4
  56.1 83.9 all-gather.6
